TPU v7x, 32 devices: a whole 2x2x4 slice. The times are simulated.
32 devices in a mesh: dp: 2 (over y), proto: 8 (over z, core), crop: 2 (over x).
Axes of the slice: x: 2, y: 2, z: 4, core: 2. Of those that a mesh axis runs over, the one named last changes fastest.
Arguments:
- embeddings: bfloat16 [256, 2, 4, 256], P(('dp', 'proto'), 'crop'), may hold values from -2 to 2
- codes: bfloat16 [256, 2, 65536], P('dp', 'crop', 'proto'), may hold values from 0 to 1, as said below
- prototypes: bfloat16 [8, 8192, 256], P('proto', ('dp', 'crop')), may hold values from -2 to 2
Outputs:
- grad_emb: float32 [256, 2, 4, 256], P(('dp', 'proto'), 'crop')
- grad_proto: float32 [8, 8192, 256], P('proto', ('dp', 'crop'))
Inputs may be any that keep to these rules, and one draw needn't show every extreme that they name: `codes`: each image's code is a distribution over the prototypes: nonnegative entries that sum to about one over all 65536.
All inputs are finite; a program needn't handle non-finite values.
Results may differ from a plain program's by a relative error of at most 0.0031.
Values may be sent and summed in bfloat16 or wider, within the bound.
A program may use at most 64 MiB of HBM per device.

v0:
```python
import jax
import jax.numpy as jnp
from jax import lax
from jax.sharding import PartitionSpec as P

sharpness_divisor = 0.1
epsilon = 1e-06


def swapped(value, axis, distance):
    mask = 2**distance
    pairs = [(source, source ^ mask) for source in range(lax.axis_size(axis))]
    return lax.ppermute(value, axis, pairs)


def normalize_rows(values):
    floats = values.astype(jnp.float32)
    lengths = jnp.sqrt(jnp.sum(floats * floats, axis=-1, keepdims=True) + epsilon)
    return (floats / lengths, lengths)


def contract_first(left, right):
    return lax.dot_general(
        left, right, (((0,), (0,)), ((), ())), preferred_element_type=jnp.float32
    )


def on_device(embeddings, codes, prototypes):
    unit_emb, emb_norm = normalize_rows(embeddings)
    rounded = unit_emb.astype(jnp.bfloat16)
    unit_proto, proto_norm = normalize_rows(prototypes[0])
    rescaled_input = lax.all_gather(
        unit_proto.astype(jnp.bfloat16), ("dp", "crop"), axis=0, tiled=True
    )
    gathered = lax.all_gather(rounded, "proto", axis=0, tiled=True)
    images = gathered.shape[0]
    crop_count = gathered.shape[2]
    features = gathered.shape[3]
    as_floats = gathered[:, 0].astype(jnp.float32)
    local_sum = jnp.sum(as_floats[:, 1:], axis=1)
    outgoing = as_floats[:, 0] + local_sum
    own_code = codes[:, 0]
    own_term = jnp.dot(own_code, rescaled_input, preferred_element_type=jnp.float32)
    incoming, other_term = swapped((outgoing, own_term), "crop", 0)
    target_sum = (local_sum + incoming).astype(jnp.bfloat16)
    view_results = jnp.where(jnp.arange(crop_count) == 0, 1.0, 2.0).astype(jnp.float32)
    block_images = min(images, 128)
    blocks = images // block_images
    row_blocks = gathered.reshape(blocks, block_images * crop_count, features)

    def block_exponent(row_block):
        prototype_scores = lax.dot_general(
            row_block, rescaled_input, (((1,), (1,)), ((), ())), preferred_element_type=jnp.float32
        )
        return jnp.exp(prototype_scores / sharpness_divisor)

    partial_totals = lax.map(
        lambda row_block: jnp.sum(block_exponent(row_block), axis=1), row_blocks
    )
    totals = lax.psum(partial_totals, "proto")
    row_weight = jnp.tile(view_results, block_images)[:, None]

    def backward_block(running, inputs):
        row_block, block_total = inputs
        probs = (block_exponent(row_block) / block_total[:, None]).astype(jnp.bfloat16)
        softened_rows = jnp.dot(probs, rescaled_input, preferred_element_type=jnp.float32)
        weighted = (row_block.astype(jnp.float32) * row_weight).astype(jnp.bfloat16)
        return (running + contract_first(probs, weighted), softened_rows)

    start_sum = jnp.zeros((rescaled_input.shape[0], features), jnp.float32)
    proto_sum, softened_rows = lax.scan(backward_block, start_sum, (row_blocks, totals))
    proto_sum = proto_sum - contract_first(own_code, target_sum)
    softened_rows = softened_rows.reshape(images, crop_count, features)
    is_global = (jnp.arange(crop_count) == 0)[None, :, None]
    assigned_code = jnp.where(
        is_global, other_term[:, None, :], (own_term + other_term)[:, None, :]
    )
    row_contributions = (
        softened_rows * view_results[None, :, None] - assigned_code
    ) / sharpness_divisor
    score_grad = lax.psum_scatter(row_contributions, "proto", scatter_dimension=0, tiled=True)[
        :, None
    ]
    grad_emb = (
        score_grad - unit_emb * jnp.sum(unit_emb * score_grad, axis=-1, keepdims=True)
    ) / emb_norm
    proto_grad = lax.psum_scatter(proto_sum, ("dp", "crop"), scatter_dimension=0, tiled=True)
    grad_proto = (
        proto_grad - unit_proto * jnp.sum(unit_proto * proto_grad, axis=-1, keepdims=True)
    ) / proto_norm
    return (grad_emb, grad_proto[None])


def solution(mesh):
    return jax.shard_map(
        on_device,
        mesh=mesh,
        in_specs=(
            P(("dp", "proto"), "crop", None, None),
            P("dp", "crop", "proto"),
            P("proto", ("dp", "crop"), None),
        ),
        out_specs=(P(("dp", "proto"), "crop", None, None), P("proto", ("dp", "crop"), None)),
        check_vma=False,
    )
```

profile of v0, /device:TPU:0, one launch (start us, length us, event | category | flops | bytes accessed | tf_op | source)
XLA Modules:
  0.0 270.6 jit_solution(16648327690122520881)
XLA Ops:
  7.2 0.0 copy-start
  7.2 0.0 copy-start.4
  7.2 0.0 all-gather.2.cloned.1.call-start
  7.2 1.7 fusion.2
  9.0 2.5 fusion.13
  11.5 0.0 all-gather.2.cloned.1.call-update
  11.5 0.0 all-reduce.3.cloned.1.call-start
  11.6 0.1 fusion.11
  11.7 0.1 fusion.12
  11.8 15.9 %all_gather.6 = bf16[128,1,4,256]{3,2,1,0:T(4,128)(2,1)S(1)} all-gather(bf16[16,1,4,256]{3,2,1,0:T(4,128)(2,1)S(1)} %fusion.12), channel_id=1, replica_groups=mesh['dp'=2,'proto'=8,'crop'=2] {'proto'}, dimensions={0}, use_global_device_ids=true | all-gather | bytes 294912 | tf_op jit(solution)/shard_map/all_gather | solution.py:35
  27.7 0.1 bitcast_convert_fusion
  27.8 0.1 slice.9
  27.9 0.4 slice_reduce_fusion
  28.2 0.7 bitcast_add_fusion
  28.9 1.5 collective-permute-start.1
  30.4 0.1 squeeze.18
  30.5 0.0 copy-start.6
  30.5 0.5 copy-done.6
  31.0 0.1 mul.57
  31.1 0.6 iota_compare_fusion
  31.7 37.7 %all-gather.2.cloned.1.call-done = bf16[8192,256]{1,0:T(8,128)(2,1)} async-done(((bf16[2048,256]{1,0:T(8,128)(2,1)}), bf16[8192,256]{1,0:T(8,128)(2,1)}) %all-gather.2.cloned.1.call-update) | async-done | bytes 4194320 | tf_op jit(solution)/shard_map/all_gather | solution.py:32
  69.4 9.3 %fusion = (f32[512]{0:T(512)S(1)}, f32[512,8192]{1,0:T(8,128)}) fusion(bf16[512,256]{1,0:T(8,128)(2,1)S(1)} %squeeze.18, bf16[8192,256]{1,0:T(8,128)(2,1)} %all-gather.2.cloned.1.call-done), kind=kOutput, calls=%fused_computation.2 | convolution fusion | flops 2155871744 | bytes 21235712 | tf_op jit(solution)/shard_map/while/body/eval_jaxpr/dot_general | solution.py:52
  78.7 16.3 %psum.7 = f32[512]{0:T(512)S(1)} all-reduce(f32[512]{0:T(512)S(1)} %get-tuple-element.21), channel_id=1, replica_groups=mesh['dp'=2,'proto'=8,'crop'=2] {'proto'}, use_global_device_ids=true, to_apply=%region_3.4 | all-reduce | flops 512 | bytes 4096 | tf_op jit(solution)/shard_map/psum | solution.py:60
  95.0 0.0 copy-done
  95.0 3.5 %fusion.6 = f32[128,256]{0,1:T(8,128)S(1)} fusion(bf16[8192,256]{1,0:T(8,128)(2,1)} %all-gather.2.cloned.1.call-done, bf16[128,1,8192]{2,0,1:T(8,128)(2,1)S(1)} %copy-done), kind=kOutput, calls=%fused_computation.13 | convolution fusion | flops 536870912 | bytes 6422528 | tf_op jit(solution)/shard_map/dot_general | solution.py:43
  98.5 1.5 collective-permute-start
  100.0 7.3 %divide_convert_fusion = bf16[512,8192]{1,0:T(8,128)(2,1)S(1)} fusion(f32[512,8192]{1,0:T(8,128)} %get-tuple-element.22, f32[512]{0:T(512)S(1)} %psum.7), kind=kLoop, calls=%fused_computation | loop fusion | flops 12582912 | bytes 25167872 | tf_op jit(solution)/shard_map/while/body/eval_jaxpr/convert_element_type | solution.py:65
  107.3 5.7 %fusion.9 = f32[8192,256]{1,0:T(8,128)} fusion(bf16[512,8192]{1,0:T(8,128)(2,1)S(1)} %divide_convert_fusion, bf16[512,256]{1,0:T(8,128)(2,1)S(1)} %squeeze.18, f32[512]{0:T(512)S(1)} %mul.57), kind=kOutput, calls=%fused_computation.17 | convolution fusion | flops 2147876864 | bytes 17041408 | tf_op jit(solution)/shard_map/while/body/eval_jaxpr/dot_general | solution.py:23
  113.0 2.3 fusion.14
  115.4 0.1 reshape.54
  115.5 0.0 collective-permute-done
  115.6 0.1 copy.12
  115.7 0.1 copy.11
  115.8 1.8 subtract_multiply_fusion
  117.5 0.0 all-reduce.3.cloned.1.call-update
  117.6 0.2 reduce-scatter.2.cloned.1.call-start
  117.8 0.0 collective-permute-done.1
  117.8 8.0 %fusion.1 = f32[8192,256]{1,0:T(8,128)} fusion(f32[8192,256]{1,0:T(8,128)} %fusion.9, bf16[128,1,8192]{2,0,1:T(8,128)(2,1)S(1)} %copy-done, f32[128,256]{1,0:T(8,128)S(1)} %slice_reduce_fusion, f32[128,256]{1,0:T(8,128)} %collective-permute-done.1), kind=kOutput, calls=%fused_computation.4 | convolution fusion | flops 539033600 | bytes 19136512 | tf_op jit(solution)/shard_map/dot_general | solution.py:23
  125.8 0.0 reduce-scatter.2.cloned.1.call-update
  125.9 0.6 copy-done.7
  126.5 0.6 dynamic-slice
  127.7 43.4 %all-reduce.3.cloned.1.call-done = f32[128,4,256]{2,1,0:T(4,128)} async-done(((f32[128,4,256]{2,1,0:T(4,128)}), f32[128,4,256]{2,1,0:T(4,128)}) %all-reduce.3.cloned.1.call-update) | async-done | bytes 524304
  171.1 0.0 copy-done.5
  171.1 1.0 multiply_reduce_fusion.1
  172.2 1.6 subtract_divide_fusion
  173.7 86.2 %reduce-scatter.2.cloned.1.call-done = f32[2048,256]{1,0:T(8,128)} async-done(((f32[8192,256]{1,0:T(8,128)}), f32[2048,256]{1,0:T(8,128)}) %reduce-scatter.2.cloned.1.call-update) | async-done | bytes 2097168 | tf_op jit(solution)/shard_map/reduce_scatter | solution.py:87
  259.9 2.4 multiply_reduce_fusion
  262.3 1.7 divide_bitcast_fusion
  (14 shorter events, 0.1 us)
Async XLA Ops:
  7.2 87.9 %copy-start = (bf16[128,1,8192]{2,0,1:T(8,128)(2,1)S(1)}, bf16[128,1,8192]{2,0,1:T(8,128)(2,1)}, u32[]{:S(2)}) copy-start(bf16[128,1,8192]{2,0,1:T(8,128)(2,1)} %param.4) | copy-start | bytes 6291460
  7.2 4.4 %copy-start.4 = (bf16[16,1,4,256]{3,2,1,0:T(4,128)(2,1)S(1)}, bf16[16,1,4,256]{3,2,1,0:T(4,128)(2,1)}, u32[]{:S(2)}) copy-start(bf16[16,1,4,256]{3,2,1,0:T(4,128)(2,1)} %param.3) | copy-start | bytes 98308
  7.2 62.2 %all-gather.2.cloned.1.call-start = ((), (), s32[]{:S(2)}) async-start(), calls=%async_computation.1 | async-start | bytes 5242880 | tf_op jit(solution)/shard_map/all_gather | solution.py:32
  11.5 159.6 %all-reduce.3.cloned.1.call-start = ((), (), s32[]{:S(2)}) async-start(), calls=%async_computation.3 | async-start | bytes 1048576
  28.9 88.9 %collective-permute-start.1 = (f32[128,256]{1,0:T(8,128)}, f32[128,256]{1,0:T(8,128)}, u32[]{:S(2)}, u32[]{:S(2)}) collective-permute-start(f32[128,256]{1,0:T(8,128)} %bitcast_add_fusion), channel_id=1, source_target_pairs={{0,1},{1,0},{2,3},{3,2},{4,5},{5,4},{6,7},{7,6},{8,9},{9,8},{10,11... | collective-permute-start | bytes 393224 | tf_op jit(solution)/shard_map/ppermute | solution.py:13
  30.5 0.5 copy-start.6
  98.5 17.0 %collective-permute-start = (f32[128,256]{0,1:T(8,128)S(1)}, f32[128,256]{0,1:T(8,128)S(1)}, u32[]{:S(2)}, u32[]{:S(2)}) collective-permute-start(f32[128,256]{0,1:T(8,128)S(1)} %fusion.6), channel_id=1, source_target_pairs={{0,1},{1,0},{2,3},{3,2},{4,5},{5,4},{6,7},{7,6},{8,9},{9,8},{10,11... | collective-permute-start | bytes 393224 | tf_op jit(solution)/shard_map/ppermute | solution.py:13
  107.3 5.7 %copy-start.2 = (bf16[8192,256]{1,0:T(8,128)(2,1)S(1)}, bf16[8192,256]{1,0:T(8,128)(2,1)}, u32[]{:S(2)}) copy-start(bf16[8192,256]{1,0:T(8,128)(2,1)} %all-gather.2.cloned.1.call-done) | copy-start | bytes 12582916
  117.6 142.4 %reduce-scatter.2.cloned.1.call-start = ((), (), s32[]{:S(2)}) async-start(), calls=%async_computation.2 | async-start | bytes 10485760 | tf_op jit(solution)/shard_map/reduce_scatter | solution.py:87
  125.8 0.7 copy-start.7
  125.8 45.3 %copy-start.5 = (bf16[16,1,4,256]{3,2,1,0:T(4,128)(2,1)S(1)}, bf16[16,1,4,256]{3,2,1,0:T(4,128)(2,1)}, u32[]{:S(2)}) copy-start(bf16[16,1,4,256]{3,2,1,0:T(4,128)(2,1)} %param.3) | copy-start | bytes 98308
  125.8 134.1 %copy-start.1 = (bf16[1,2048,256]{2,1,0:T(8,128)(2,1)S(1)}, bf16[1,2048,256]{2,1,0:T(8,128)(2,1)}, u32[]{:S(2)}) copy-start(bf16[1,2048,256]{2,1,0:T(8,128)(2,1)} %param.5) | copy-start | bytes 3145732
  259.9 2.4 copy-start.3
Sparse Core Ops, SparseCore 0:
  11.7 57.6 all-gather.1
  117.7 53.4 all-reduce.2
  174.5 85.3 reduce-scatter.1
where the time goes:
time: 271 us
  waiting for transfers between devices  167 us (62%)
  blocking collectives  32.2 us (12%)
  matrix products  28.8 us (11%)
  other arithmetic  21.9 us (8%)
  between operations  14.6 us (5%)
  starting transfers between devices  3.33 us (1%)
    reduce_scatter x1, waiting for transfers between devices, on_device(): lax.psum_scatter(proto_sum, ('dp', 'crop'), scatter_dimension=0, tiled=True)  86.2 us
    unnamed x4, waiting for transfers between devices  43.5 us
    all_gather x1, waiting for transfers between devices, on_device(): lax.all_gather(unit_proto.astype(jnp.bfloat16), ('dp', 'crop'), axis=0, t...  37.7 us
    psum x1, blocking collectives, on_device(): totals = lax.psum(partial_totals, 'proto')  16.3 us
    all_gather x1, blocking collectives, on_device(): gathered = lax.all_gather(rounded, 'proto', axis=0, tiled=True)  15.9 us
    dot_general x2, matrix products, contract_first(): lax.dot_general(left, right, (((0,), (0,)), ((), ())), preferred_element_...  13.8 us
    dot_general x1, matrix products, block_exponent(): lax.dot_general(row_block, rescaled_input, (((1,), (1,)), ((), ())), pref...  9.3 us
    convert_element_type x1, other arithmetic, backward_block(): (block_exponent(row_block) / block_total[:, None]).astype(jnp.bfloat16)  7.27 us
  transfers between devices with their start and end apart: 5, of which 3 were waited for; matrix products, arithmetic and copies ran while one was open for 16% of the time, Pallas kernels for 0%

commit v1 on v0

v1 whole, which is shorter than its diff:
```python
import functools

import jax
import jax.numpy as jnp
from jax import lax
from jax.experimental import pallas as pl
from jax.experimental.pallas import tpu as pltpu
from jax.sharding import PartitionSpec as P

sharpness = 10.0
epsilon = 1e-06
MESH = pl.DeviceIdType.MESH


def unit_rows(values):
    floats = values.astype(jnp.float32)
    lengths = jnp.sqrt(jnp.sum(floats * floats, axis=-1, keepdims=True) + epsilon)
    return floats / lengths, lengths


def kernel(
    sizes,
    emb_ref,
    codes_ref,
    proto_ref,
    gemb_ref,
    gproto_ref,
    z_all,
    c_all,
    c_buf,
    ct_buf,
    e_all,
    tot_buf,
    tot_in1,
    tot_mid,
    tot_in2,
    rc_buf,
    cp_buf,
    ts_buf,
    rs1_in,
    rs2_out,
    rs2_in,
    rs3_out,
    rs3_in,
    s1_send,
    s1_recv,
    s2_send,
    s2_recv,
    s3_send,
    s3_recv,
    code_send,
    code_recv,
    code_local,
    t1_send,
    t1_recv,
    t2_send,
    t2_recv,
    r1_send,
    r1_recv,
    r2_send,
    r2_recv,
    r3_send,
    r3_recv,
):
    n_dp, n_proto, n_crop, images, crops, tile = sizes
    n_plane, n_z = n_dp * n_crop, n_proto // 2
    shard = images * crops
    unit = n_z * shard
    group = n_proto * images
    owned = proto_ref.shape[0]
    tiles = owned // tile

    my_dp, my_proto, my_crop = (lax.axis_index(a) for a in ("dp", "proto", "crop"))
    plane = my_dp * n_crop + my_crop
    zi, core = my_proto // 2, my_proto % 2
    sibling = {"proto": zi * 2 + (1 - core)}

    def plane_peer(d):
        q = lax.rem(plane + d, n_plane)
        return q, {"dp": q // n_crop, "crop": q % n_crop}

    def plane_from(d):
        return lax.rem(plane + n_plane - d, n_plane)

    def z_peer(d):
        other = lax.rem(zi + d, n_z)
        return other, {"proto": other * 2 + core}

    def proto_peer(d):
        return {"proto": lax.rem(my_proto + d, n_proto)}

    def remote(src, dst, send, recv, device):
        return pltpu.make_async_remote_copy(
            src_ref=src, dst_ref=dst, send_sem=send, recv_sem=recv,
            device_id=device, device_id_type=MESH,
        )

    barrier = pltpu.get_barrier_semaphore()
    for d in range(1, n_proto):
        pl.semaphore_signal(barrier, inc=1, device_id=proto_peer(d), device_id_type=MESH)
    for d in range(1, n_plane):
        pl.semaphore_signal(barrier, inc=1, device_id=plane_peer(d)[1], device_id_type=MESH)

    own_codes = pltpu.make_async_copy(
        codes_ref.at[:, pl.ds(pl.multiple_of(plane * owned, owned), owned)],
        c_all.at[pl.ds(pl.multiple_of(plane * group, group), group), :],
        code_local,
    )
    own_codes.start()
    own_rows = pl.ds(pl.multiple_of(zi * shard, shard), shard)
    z_all[core, plane, own_rows, :] = unit_rows(emb_ref[...])[0].astype(jnp.bfloat16)

    pl.semaphore_wait(barrier, n_proto - 1 + n_plane - 1)

    sent = []
    s1 = []
    for d in range(1, n_z):
        ref = z_all.at[core, plane, own_rows, :]
        s1.append(remote(ref, ref, s1_send.at[d - 1], s1_recv.at[d - 1], z_peer(d)[1]))
        s1[-1].start()

    def tile_rows(t):
        return pl.ds(pl.multiple_of(t * tile, tile), tile)

    def normalize_tile(t, carry):
        unit_w = unit_rows(proto_ref[tile_rows(t), :])[0]
        c_buf[tile_rows(t), :] = unit_w.astype(jnp.bfloat16)
        ct_buf[:, tile_rows(t)] = unit_w.T.astype(jnp.bfloat16)
        return carry

    lax.fori_loop(0, tiles, normalize_tile, 0)

    for copy in s1:
        copy.wait_recv()
    s2 = []
    for d in range(1, n_plane):
        ref = z_all.at[core, plane]
        s2.append(remote(ref, ref, s2_send.at[d - 1], s2_recv.at[d - 1], plane_peer(d)[1]))
        s2[-1].start()
    code_copies = []
    for d in range(1, n_plane):
        q, device = plane_peer(d)
        code_copies.append(remote(
            codes_ref.at[:, pl.ds(pl.multiple_of(q * owned, owned), owned)],
            c_all.at[pl.ds(pl.multiple_of(plane * group, group), group), :],
            code_send.at[d - 1], code_recv.at[d - 1], device,
        ))
        code_copies[-1].start()
    sent += code_copies

    def score_unit(half, q):
        rows = z_all[half, q]

        def score_tile(t, sums):
            scores = lax.dot_general(
                c_buf[tile_rows(t), :], rows, (((1,), (1,)), ((), ())),
                preferred_element_type=jnp.float32,
            )
            exponent = jnp.exp(scores * sharpness)
            e_all[half * n_plane + q, tile_rows(t), :] = exponent.astype(jnp.bfloat16)
            return sums + jnp.sum(exponent, axis=0, keepdims=True)

        sums = lax.fori_loop(0, tiles, score_tile, jnp.zeros((1, unit), jnp.float32))
        tot_buf[pl.ds(half * n_plane + q, 1), :] = sums

    s3 = []
    for d in range(n_plane):
        q = plane_from(d)
        if d:
            s2[d - 1].wait_recv()
        ref = z_all.at[core, q]
        s3.append(remote(ref, ref, s3_send.at[d], s3_recv.at[d], sibling))
        s3[-1].start()
        score_unit(core, q)
    for d in range(n_plane):
        s3[d].wait_recv()
        score_unit(1 - core, plane_from(d))

    t1 = []
    for d in range(1, n_proto):
        t1.append(remote(
            tot_buf, tot_in1.at[d - 1], t1_send.at[d - 1], t1_recv.at[d - 1], proto_peer(d)
        ))
        t1[-1].start()

    def soften_unit(u, carry):
        columns = jnp.dot(ct_buf[...], e_all[u], preferred_element_type=jnp.float32)
        rc_buf[u] = columns.T
        return carry

    lax.fori_loop(0, 2 * n_plane, soften_unit, 0)

    total = tot_buf[...]
    for d in range(1, n_proto):
        t1[d - 1].wait_recv()
        total = total + tot_in1[d - 1]
    tot_mid[...] = total
    t2 = []
    for d in range(1, n_plane):
        t2.append(remote(
            tot_mid, tot_in2.at[d - 1], t2_send.at[d - 1], t2_recv.at[d - 1], plane_peer(d)[1]
        ))
        t2[-1].start()
    sent += t2

    def image_rows(half, z):
        return pl.ds((z * 2 + half) * images, images)

    def crop_rows(z, v):
        return pl.ds(z * shard + v * images, images)

    def target_group(a, carry):
        for half in range(2):
            for z in range(n_z):
                locals_sum = None
                for g in range(n_crop):
                    for v in range(1, crops):
                        term = z_all[half, a * n_crop + g, crop_rows(z, v), :].astype(jnp.float32)
                        locals_sum = term if locals_sum is None else locals_sum + term
                for t in range(n_crop):
                    other = z_all[half, a * n_crop + 1 - t, crop_rows(z, 0), :]
                    ts_buf[a, t, image_rows(half, z), :] = (
                        locals_sum + other.astype(jnp.float32)
                    ).astype(jnp.bfloat16)
        return carry

    lax.fori_loop(0, n_dp, target_group, 0)

    own_codes.wait()
    for copy in code_copies:
        copy.wait_recv()

    def code_products(q, carry):
        rows = pl.ds(pl.multiple_of(q * group, group), group)
        cp_buf[q] = jnp.dot(c_all[rows, :], c_buf[...], preferred_element_type=jnp.float32)
        return carry

    lax.fori_loop(0, n_plane, code_products, 0)

    total = tot_mid[...]
    for d in range(1, n_plane):
        t2[d - 1].wait_recv()
        total = total + tot_in2[d - 1]
    crop_of = lax.rem(lax.broadcasted_iota(jnp.int32, total.shape, 1) // images, crops)
    tot_buf_weights = jnp.where(crop_of == 0, 1.0, 2.0) / total
    for copy in t1 + s1 + s2 + s3:
        copy.wait_send()
    tot_buf[...] = tot_buf_weights

    lanes = 128

    def row_unit(half, q):
        u = half * n_plane + q
        weights = tot_buf[pl.ds(u, 1), :]
        a, g = q // n_crop, q % n_crop
        for b in range(unit // lanes):
            part = pl.ds(b * lanes, lanes)
            column = jnp.broadcast_to(weights[:, b * lanes:(b + 1) * lanes], (lanes, lanes)).T
            column = jnp.concatenate([column] * (z_all.shape[-1] // lanes), axis=1)
            z_all[half, q, part, :] = (
                z_all[half, q, part, :].astype(jnp.float32) * column
            ).astype(jnp.bfloat16)
            rc_buf[u, part, :] = rc_buf[u, part, :] * column
        for z in range(n_z):
            rows = pl.ds(pl.multiple_of((z * 2 + half) * images, images), images)
            other = cp_buf[a * n_crop + 1 - g, rows, :]
            both = other + cp_buf[q, rows, :]
            for v in range(crops):
                code_term = other if v == 0 else both
                rc_buf[u, crop_rows(z, v), :] = (
                    rc_buf[u, crop_rows(z, v), :] - code_term
                ) * sharpness

    r1 = []
    for d in range(n_plane):
        q = plane_from(d)
        row_unit(1 - core, q)
        r1.append(remote(
            rc_buf.at[(1 - core) * n_plane + q], rs1_in.at[q],
            r1_send.at[d], r1_recv.at[d], sibling,
        ))
        r1[-1].start()
    sent += r1
    for d in range(n_plane):
        row_unit(core, plane_from(d))

    r2 = []
    for d in range(n_plane):
        r1[d].wait_recv()
        q = plane_from(d)
        if d == 0:
            continue
        rs2_out[d - 1] = (rc_buf[core * n_plane + q] + rs1_in[q]).astype(jnp.bfloat16)
        device = {"dp": q // n_crop, "crop": q % n_crop}
        r2.append(remote(
            rs2_out.at[d - 1], rs2_in.at[d - 1], r2_send.at[d - 1], r2_recv.at[d - 1], device
        ))
        r2[-1].start()
    sent += r2

    def proto_tile(t, carry):
        rows = tile_rows(t)
        grad = jnp.dot(e_all[0, rows, :], z_all[0, 0], preferred_element_type=jnp.float32)
        for u in range(1, 2 * n_plane):
            grad = grad + jnp.dot(
                e_all[u, rows, :], z_all[u // n_plane, u % n_plane], preferred_element_type=jnp.float32
            )
        targets = ts_buf[...].reshape(n_plane * group, ts_buf.shape[-1])
        grad = grad - lax.dot_general(
            c_all[:, rows], targets, (((0,), (0,)), ((), ())), preferred_element_type=jnp.float32
        )
        unit_w, length = unit_rows(proto_ref[rows, :])
        along = jnp.sum(unit_w * grad, axis=-1, keepdims=True)
        gproto_ref[rows, :] = (grad - unit_w * along) / length
        return carry

    first = tiles // 2
    lax.fori_loop(0, first, proto_tile, 0)

    rows_sum = rc_buf[core * n_plane + plane] + rs1_in[plane]
    for copy in r2:
        copy.wait_recv()
    for d in range(1, n_plane):
        rows_sum = rows_sum + rs2_in[d - 1].astype(jnp.float32)
    rs3_out[...] = rows_sum
    r3 = []
    for d in range(1, n_z):
        other, device = z_peer(d)
        r3.append(remote(
            rs3_out.at[pl.ds(pl.multiple_of(other * shard, shard), shard), :], rs3_in.at[d - 1],
            r3_send.at[d - 1], r3_recv.at[d - 1], device,
        ))
        r3[-1].start()
    sent += r3

    lax.fori_loop(first, tiles, proto_tile, 0)

    score_grad = rs3_out[own_rows, :]
    for d in range(1, n_z):
        r3[d - 1].wait_recv()
        score_grad = score_grad + rs3_in[d - 1]
    unit_e, length = unit_rows(emb_ref[...])
    along = jnp.sum(unit_e * score_grad, axis=-1, keepdims=True)
    gemb_ref[...] = (score_grad - unit_e * along) / length
    for copy in sent:
        copy.wait_send()


def on_device(sizes, embeddings, codes, prototypes):
    n_dp, n_proto, n_crop = sizes
    images, _, crops, features = embeddings.shape
    owned = prototypes.shape[1]
    n_plane, n_z = n_dp * n_crop, n_proto // 2
    shard = images * crops
    unit = n_z * shard
    group = codes.shape[0]
    units = 2 * n_plane
    tile = min(owned, 256)
    rows = embeddings[:, 0].transpose(1, 0, 2).reshape(shard, features)
    vmem = pl.BlockSpec(memory_space=pltpu.VMEM)
    dma = pltpu.SemaphoreType.DMA
    bf16, f32 = jnp.bfloat16, jnp.float32
    pairs = [n_z - 1, n_plane - 1, n_plane, n_plane - 1]
    sems = []
    for count in pairs:
        sems += [dma((max(count, 1),)), dma((max(count, 1),))]
    sems.append(dma)
    for count in (n_proto - 1, n_plane - 1, n_plane, n_plane - 1, n_z - 1):
        sems += [dma((max(count, 1),)), dma((max(count, 1),))]
    grad_emb, grad_proto = pl.pallas_call(
        functools.partial(kernel, (n_dp, n_proto, n_crop, images, crops, tile)),
        out_shape=(
            jax.ShapeDtypeStruct((shard, features), f32),
            jax.ShapeDtypeStruct((owned, features), f32),
        ),
        in_specs=[vmem, pl.BlockSpec(memory_space=pl.ANY), vmem],
        out_specs=(vmem, vmem),
        scratch_shapes=[
            pltpu.VMEM((2, n_plane, unit, features), bf16),
            pltpu.VMEM((n_plane * group, owned), bf16),
            pltpu.VMEM((owned, features), bf16),
            pltpu.VMEM((features, owned), bf16),
            pltpu.VMEM((units, owned, unit), bf16),
            pltpu.VMEM((units, unit), f32),
            pltpu.VMEM((n_proto - 1, units, unit), f32),
            pltpu.VMEM((units, unit), f32),
            pltpu.VMEM((max(n_plane - 1, 1), units, unit), f32),
            pltpu.VMEM((units, unit, features), f32),
            pltpu.VMEM((n_plane, group, features), f32),
            pltpu.VMEM((n_dp, n_crop, group, features), bf16),
            pltpu.VMEM((n_plane, unit, features), f32),
            pltpu.VMEM((max(n_plane - 1, 1), unit, features), bf16),
            pltpu.VMEM((max(n_plane - 1, 1), unit, features), bf16),
            pltpu.VMEM((unit, features), f32),
            pltpu.VMEM((max(n_z - 1, 1), shard, features), f32),
        ] + sems,
        compiler_params=pltpu.CompilerParams(
            collective_id=0, has_side_effects=True, vmem_limit_bytes=62 * 2**20
        ),
        cost_estimate=pl.CostEstimate(
            flops=6 * units * unit * owned * features, bytes_accessed=8 * owned * features,
            transcendentals=units * unit * owned,
        ),
    )(rows, codes[:, 0], prototypes[0])
    grad_emb = grad_emb.reshape(crops, images, features).transpose(1, 0, 2)
    return grad_emb[:, None], grad_proto[None]


def solution(mesh):
    sizes = tuple(mesh.shape[a] for a in ("dp", "proto", "crop"))
    return jax.shard_map(
        functools.partial(on_device, sizes),
        mesh=mesh,
        in_specs=(
            P(("dp", "proto"), "crop", None, None),
            P("dp", "crop", "proto"),
            P("proto", ("dp", "crop"), None),
        ),
        out_specs=(P(("dp", "proto"), "crop", None, None), P("proto", ("dp", "crop"), None)),
        check_vma=False,
    )
```

time: 271 us -> 73.6 us (0.27)
  waiting for transfers between devices: 167 us -> 0 us
  Pallas kernels: 0 us -> 66.8 us
  blocking collectives: 32.2 us -> 0 us
  matrix products: 28.8 us -> 0 us
  other arithmetic: 21.9 us -> 0 us
  between operations: 14.6 us -> 0.64 us
  local copies, waits for them, and re-layouts: 2.35 us -> 5.94 us
  starting transfers between devices: 3.33 us -> 0 us
    reduce_scatter x1 -> x0, waiting for transfers between devices: 86.2 us -> none  [on_device(): lax.psum_scatter(proto_sum, ('dp', 'crop'), scatter_dimension=0, tiled=True)]
    pallas_call x0 -> x1, Pallas kernels: none -> 66.8 us  [on_device(): pl.pallas_call(functools.partial(kernel, (n_dp, n_proto, n_crop, images,...]
    unnamed x4 -> x0, waiting for transfers between devices: 43.5 us -> none
    all_gather x1 -> x0, waiting for transfers between devices: 37.7 us -> none  [on_device(): lax.all_gather(unit_proto.astype(jnp.bfloat16), ('dp', 'crop'), axis=0, t...]
    dot_general x5 -> x0, matrix products: 28.8 us -> none  [the longest x2 13.8 us: contract_first(): lax.dot_general(left, right, (((0,), (0,)), ((), ())), preferred_element_...]
    psum x1 -> x0, blocking collectives: 16.3 us -> none  [on_device(): totals = lax.psum(partial_totals, 'proto')]
    all_gather x1 -> x0, blocking collectives: 15.9 us -> none  [on_device(): gathered = lax.all_gather(rounded, 'proto', axis=0, tiled=True)]
    convert_element_type x4 -> x0, other arithmetic: 9.97 us -> none  [the longest x1 7.27 us: backward_block(): (block_exponent(row_block) / block_total[:, None]).astype(jnp.bfloat16)]
  transfers between devices with their start and end apart: 5 -> 0, of which waited for: 3 -> 0; matrix products, arithmetic and copies ran while one was open for 16% -> 0% of each run, Pallas kernels for 0% -> 0%
where the time goes in v1:
time: 73.6 us; the launch traced here: 73.3 us
  Pallas kernels  66.8 us (91%)
  local copies, waits for them, and re-layouts  5.94 us (8%)
    pallas_call x1, Pallas kernels, on_device(): pl.pallas_call(functools.partial(kernel, (n_dp, n_proto, n_crop, images,...  66.8 us
    unnamed x1, local copies, waits for them, and re-layouts  3.04 us
    reshape x1, local copies, waits for them, and re-layouts, on_device(): grad_emb = grad_emb.reshape(crops, images, features).transpose(1, 0, 2)  1.51 us

profile of v1, /device:TPU:0, one launch (start us, length us, event | category | flops | bytes accessed | tf_op | source)
XLA Modules:
  0.0 73.3 jit_solution(8424530232785323995)
XLA Ops:
  0.6 1.4 %copy.5 = bf16[4,16,256]{2,1,0:T(8,128)(2,1)} copy(bf16[4,16,256]{2,0,1:T(4,128)(2,1)} %bitcast.16) | data formatting | bytes 65536 | tf_op jit(solution)/shard_map/transpose | solution.py:359
  2.0 66.8 %shard_map.50 = (f32[64,256]{1,0:T(8,128)}, f32[2048,256]{1,0:T(8,128)}) custom-call(bf16[64,256]{1,0:T(8,128)(2,1)} %bitcast.17, bf16[128,8192]{1,0:T(8,128)(2,1)} %bitcast.18, bf16[2048,256]{1,0:T(8,128)(2,1)} %bitcast.19), custom_call_target="tpu_custom_call" | custom-call | flops 6442450944 | bytes 4194304 | tf_op jit(solution)/shard_map/pallas_call | solution.py:370
  68.8 1.5 %copy.8 = f32[4,16,256]{2,0,1:T(4,128)} copy(f32[4,16,256]{2,1,0:T(8,128)} %bitcast.15) | data formatting | bytes 131072 | tf_op jit(solution)/shard_map/reshape | solution.py:405
  70.3 3.0 %copy.10 = f32[1,2048,256]{2,1,0:T(8,128)} copy(f32[1,2048,256]{2,1,0:T(8,128)} %bitcast.13) | data formatting | bytes 4194304

commit v2 on v1

--- a/solution.py
+++ b/solution.py
@@ -107,8 +107,11 @@
         code_local,
     )
     own_codes.start()
+    emb_floats = emb_ref[...].astype(jnp.float32)
+    emb_rows = jnp.concatenate([emb_floats[:, v, :] for v in range(crops)], axis=0)
+    unit_e, emb_length = unit_rows(emb_rows)
     own_rows = pl.ds(pl.multiple_of(zi * shard, shard), shard)
-    z_all[core, plane, own_rows, :] = unit_rows(emb_ref[...])[0].astype(jnp.bfloat16)
+    z_all[core, plane, own_rows, :] = unit_e.astype(jnp.bfloat16)
 
     pl.semaphore_wait(barrier, n_proto - 1 + n_plane - 1)
 
@@ -119,6 +122,18 @@
         s1.append(remote(ref, ref, s1_send.at[d - 1], s1_recv.at[d - 1], z_peer(d)[1]))
         s1[-1].start()
 
+    s2 = {}
+
+    def send_shard(dz):
+        source = lax.rem(zi + n_z - dz, n_z)
+        ref = z_all.at[core, plane, pl.ds(pl.multiple_of(source * shard, shard), shard), :]
+        for d in range(1, n_plane):
+            sem = dz * (n_plane - 1) + d - 1
+            s2[dz, d] = remote(ref, ref, s2_send.at[sem], s2_recv.at[sem], plane_peer(d)[1])
+            s2[dz, d].start()
+
+    send_shard(0)
+
     def tile_rows(t):
         return pl.ds(pl.multiple_of(t * tile, tile), tile)
 
@@ -128,15 +143,11 @@
         ct_buf[:, tile_rows(t)] = unit_w.T.astype(jnp.bfloat16)
         return carry
 
-    lax.fori_loop(0, tiles, normalize_tile, 0)
-
-    for copy in s1:
-        copy.wait_recv()
-    s2 = []
-    for d in range(1, n_plane):
-        ref = z_all.at[core, plane]
-        s2.append(remote(ref, ref, s2_send.at[d - 1], s2_recv.at[d - 1], plane_peer(d)[1]))
-        s2[-1].start()
+    lax.fori_loop(0, tiles, normalize_tile, 0, unroll=True)
+
+    for dz in range(1, n_z):
+        s1[dz - 1].wait_recv()
+        send_shard(dz)
     code_copies = []
     for d in range(1, n_plane):
         q, device = plane_peer(d)
@@ -160,18 +171,25 @@
             e_all[half * n_plane + q, tile_rows(t), :] = exponent.astype(jnp.bfloat16)
             return sums + jnp.sum(exponent, axis=0, keepdims=True)
 
-        sums = lax.fori_loop(0, tiles, score_tile, jnp.zeros((1, unit), jnp.float32))
+        sums = lax.fori_loop(
+            0, tiles, score_tile, jnp.zeros((1, unit), jnp.float32), unroll=True
+        )
         tot_buf[pl.ds(half * n_plane + q, 1), :] = sums
+
+    def soften_unit(u):
+        columns = jnp.dot(ct_buf[...], e_all[u], preferred_element_type=jnp.float32)
+        rc_buf[u] = columns.T
 
     s3 = []
     for d in range(n_plane):
         q = plane_from(d)
-        if d:
-            s2[d - 1].wait_recv()
+        for dz in range(n_z if d else 0):
+            s2[dz, d].wait_recv()
         ref = z_all.at[core, q]
         s3.append(remote(ref, ref, s3_send.at[d], s3_recv.at[d], sibling))
         s3[-1].start()
         score_unit(core, q)
+        soften_unit(core * n_plane + q)
     for d in range(n_plane):
         s3[d].wait_recv()
         score_unit(1 - core, plane_from(d))
@@ -183,12 +201,8 @@
         ))
         t1[-1].start()
 
-    def soften_unit(u, carry):
-        columns = jnp.dot(ct_buf[...], e_all[u], preferred_element_type=jnp.float32)
-        rc_buf[u] = columns.T
-        return carry
-
-    lax.fori_loop(0, 2 * n_plane, soften_unit, 0)
+    for d in range(n_plane):
+        soften_unit((1 - core) * n_plane + plane_from(d))
 
     total = tot_buf[...]
     for d in range(1, n_proto):
@@ -230,12 +244,17 @@
     for copy in code_copies:
         copy.wait_recv()
 
-    def code_products(q, carry):
-        rows = pl.ds(pl.multiple_of(q * group, group), group)
-        cp_buf[q] = jnp.dot(c_all[rows, :], c_buf[...], preferred_element_type=jnp.float32)
+    code_rows = n_plane * group
+    chunk = min(code_rows, 512)
+
+    def code_products(k, carry):
+        rows = pl.ds(pl.multiple_of(k * chunk, chunk), chunk)
+        cp_buf[rows, :] = jnp.dot(
+            c_all[rows, :], c_buf[...], preferred_element_type=jnp.float32
+        )
         return carry
 
-    lax.fori_loop(0, n_plane, code_products, 0)
+    lax.fori_loop(0, code_rows // chunk, code_products, 0)
 
     total = tot_mid[...]
     for d in range(1, n_plane):
@@ -243,7 +262,7 @@
         total = total + tot_in2[d - 1]
     crop_of = lax.rem(lax.broadcasted_iota(jnp.int32, total.shape, 1) // images, crops)
     tot_buf_weights = jnp.where(crop_of == 0, 1.0, 2.0) / total
-    for copy in t1 + s1 + s2 + s3:
+    for copy in t1 + s1 + list(s2.values()) + s3:
         copy.wait_send()
     tot_buf[...] = tot_buf_weights
 
@@ -262,32 +281,35 @@
             ).astype(jnp.bfloat16)
             rc_buf[u, part, :] = rc_buf[u, part, :] * column
         for z in range(n_z):
-            rows = pl.ds(pl.multiple_of((z * 2 + half) * images, images), images)
-            other = cp_buf[a * n_crop + 1 - g, rows, :]
-            both = other + cp_buf[q, rows, :]
+            def code_part(t):
+                start = (a * n_crop + t) * group + (z * 2 + half) * images
+                return cp_buf[pl.ds(pl.multiple_of(start, images), images), :]
+
+            other = code_part(1 - g)
+            both = other + code_part(g)
             for v in range(crops):
                 code_term = other if v == 0 else both
                 rc_buf[u, crop_rows(z, v), :] = (
                     rc_buf[u, crop_rows(z, v), :] - code_term
                 ) * sharpness
 
-    r1 = []
-    for d in range(n_plane):
+    r1 = {}
+    order = list(range(1, n_plane)) + [0]
+    for d in order:
         q = plane_from(d)
         row_unit(1 - core, q)
-        r1.append(remote(
+        r1[d] = remote(
             rc_buf.at[(1 - core) * n_plane + q], rs1_in.at[q],
             r1_send.at[d], r1_recv.at[d], sibling,
-        ))
-        r1[-1].start()
-    sent += r1
-    for d in range(n_plane):
-        row_unit(core, plane_from(d))
+        )
+        r1[d].start()
+    sent += list(r1.values())
 
     r2 = []
-    for d in range(n_plane):
+    for d in order:
+        q = plane_from(d)
+        row_unit(core, q)
         r1[d].wait_recv()
-        q = plane_from(d)
         if d == 0:
             continue
         rs2_out[d - 1] = (rc_buf[core * n_plane + q] + rs1_in[q]).astype(jnp.bfloat16)
@@ -298,13 +320,13 @@
         r2[-1].start()
     sent += r2
 
+    wide = min(owned, 2 * tile)
+
     def proto_tile(t, carry):
-        rows = tile_rows(t)
-        grad = jnp.dot(e_all[0, rows, :], z_all[0, 0], preferred_element_type=jnp.float32)
-        for u in range(1, 2 * n_plane):
-            grad = grad + jnp.dot(
-                e_all[u, rows, :], z_all[u // n_plane, u % n_plane], preferred_element_type=jnp.float32
-            )
+        rows = pl.ds(pl.multiple_of(t * wide, wide), wide)
+        exponents = jnp.concatenate([e_all[u, rows, :] for u in range(2 * n_plane)], axis=1)
+        weighted = z_all[...].reshape(2 * n_plane * unit, z_all.shape[-1])
+        grad = jnp.dot(exponents, weighted, preferred_element_type=jnp.float32)
         targets = ts_buf[...].reshape(n_plane * group, ts_buf.shape[-1])
         grad = grad - lax.dot_general(
             c_all[:, rows], targets, (((0,), (0,)), ((), ())), preferred_element_type=jnp.float32
@@ -314,7 +336,7 @@
         gproto_ref[rows, :] = (grad - unit_w * along) / length
         return carry
 
-    first = tiles // 2
+    first = (owned // wide) * 3 // 4
     lax.fori_loop(0, first, proto_tile, 0)
 
     rows_sum = rc_buf[core * n_plane + plane] + rs1_in[plane]
@@ -333,15 +355,16 @@
         r3[-1].start()
     sent += r3
 
-    lax.fori_loop(first, tiles, proto_tile, 0)
+    lax.fori_loop(first, owned // wide, proto_tile, 0)
 
     score_grad = rs3_out[own_rows, :]
     for d in range(1, n_z):
         r3[d - 1].wait_recv()
         score_grad = score_grad + rs3_in[d - 1]
-    unit_e, length = unit_rows(emb_ref[...])
     along = jnp.sum(unit_e * score_grad, axis=-1, keepdims=True)
-    gemb_ref[...] = (score_grad - unit_e * along) / length
+    grad_rows = (score_grad - unit_e * along) / emb_length
+    for v in range(crops):
+        gemb_ref[:, v, :] = grad_rows[v * images:(v + 1) * images]
     for copy in sent:
         copy.wait_send()
 
@@ -356,11 +379,10 @@
     group = codes.shape[0]
     units = 2 * n_plane
     tile = min(owned, 256)
-    rows = embeddings[:, 0].transpose(1, 0, 2).reshape(shard, features)
     vmem = pl.BlockSpec(memory_space=pltpu.VMEM)
     dma = pltpu.SemaphoreType.DMA
     bf16, f32 = jnp.bfloat16, jnp.float32
-    pairs = [n_z - 1, n_plane - 1, n_plane, n_plane - 1]
+    pairs = [n_z - 1, n_z * (n_plane - 1), n_plane, n_plane - 1]
     sems = []
     for count in pairs:
         sems += [dma((max(count, 1),)), dma((max(count, 1),))]
@@ -370,7 +392,7 @@
     grad_emb, grad_proto = pl.pallas_call(
         functools.partial(kernel, (n_dp, n_proto, n_crop, images, crops, tile)),
         out_shape=(
-            jax.ShapeDtypeStruct((shard, features), f32),
+            jax.ShapeDtypeStruct((images, crops, features), f32),
             jax.ShapeDtypeStruct((owned, features), f32),
         ),
         in_specs=[vmem, pl.BlockSpec(memory_space=pl.ANY), vmem],
@@ -386,7 +408,7 @@
             pltpu.VMEM((units, unit), f32),
             pltpu.VMEM((max(n_plane - 1, 1), units, unit), f32),
             pltpu.VMEM((units, unit, features), f32),
-            pltpu.VMEM((n_plane, group, features), f32),
+            pltpu.VMEM((n_plane * group, features), f32),
             pltpu.VMEM((n_dp, n_crop, group, features), bf16),
             pltpu.VMEM((n_plane, unit, features), f32),
             pltpu.VMEM((max(n_plane - 1, 1), unit, features), bf16),
@@ -401,8 +423,7 @@
             flops=6 * units * unit * owned * features, bytes_accessed=8 * owned * features,
             transcendentals=units * unit * owned,
         ),
-    )(rows, codes[:, 0], prototypes[0])
-    grad_emb = grad_emb.reshape(crops, images, features).transpose(1, 0, 2)
+    )(embeddings[:, 0], codes[:, 0], prototypes[0])
     return grad_emb[:, None], grad_proto[None]
 
 

time: 73.6 us -> 62.8 us (0.85)
  Pallas kernels: 66.8 us -> 57.4 us
  local copies, waits for them, and re-layouts: 5.94 us -> 4.52 us
    pallas_call x1, Pallas kernels: 66.8 us -> 57.4 us  [on_device(): pl.pallas_call(functools.partial(kernel, (n_dp, n_proto, n_crop, images,...]
    reshape x1 -> x0, local copies, waits for them, and re-layouts: 1.51 us -> none  [on_device(): grad_emb = grad_emb.reshape(crops, images, features).transpose(1, 0, 2)]
    unnamed x1 -> x2, local copies, waits for them, and re-layouts: 3.04 us -> 4.52 us
    transpose x1 -> x0, local copies, waits for them, and re-layouts: 1.38 us -> none  [on_device(): rows = embeddings[:, 0].transpose(1, 0, 2).reshape(shard, features)]
where the time goes in v2:
time: 62.8 us; the launch traced here: 62.6 us
  Pallas kernels  57.4 us (91%)
  local copies, waits for them, and re-layouts  4.52 us (7%)
  between operations  0.64 us (1%)
    pallas_call x1, Pallas kernels, on_device(): pl.pallas_call(functools.partial(kernel, (n_dp, n_proto, n_crop, images,...  57.4 us
    unnamed x2, local copies, waits for them, and re-layouts  4.52 us

profile of v2, /device:TPU:0, one launch (start us, length us, event | category | flops | bytes accessed | tf_op | source)
XLA Modules:
  0.0 62.6 jit_solution(417848806281207255)
XLA Ops:
  0.6 57.4 %shard_map.50 = (f32[16,4,256]{2,1,0:T(4,128)}, f32[2048,256]{1,0:T(8,128)}) custom-call(bf16[16,4,256]{2,1,0:T(4,128)(2,1)} %bitcast.11, bf16[128,8192]{1,0:T(8,128)(2,1)} %bitcast.9, bf16[2048,256]{1,0:T(8,128)(2,1)} %bitcast.10), custom_call_target="tpu_custom_call" | custom-call | flops 6442450944 | bytes 4194304 | tf_op jit(solution)/shard_map/pallas_call | solution.py:392
  58.0 1.5 %copy.8 = f32[16,1,4,256]{3,2,1,0:T(4,128)} copy(f32[16,1,4,256]{3,2,1,0:T(4,128)} %bitcast.8) | data formatting | bytes 131072
  59.5 3.0 %copy.9 = f32[1,2048,256]{2,1,0:T(8,128)} copy(f32[1,2048,256]{2,1,0:T(8,128)} %bitcast.7) | data formatting | bytes 4194304

commit v3 on v2

--- a/solution.py
+++ b/solution.py
@@ -1,4 +1,5 @@
 import functools
+import math
 
 import jax
 import jax.numpy as jnp
@@ -25,6 +26,8 @@
     proto_ref,
     gemb_ref,
     gproto_ref,
+    gp_buf,
+    gp_sem,
     z_all,
     c_all,
     c_buf,
@@ -133,21 +136,6 @@
             s2[dz, d].start()
 
     send_shard(0)
-
-    def tile_rows(t):
-        return pl.ds(pl.multiple_of(t * tile, tile), tile)
-
-    def normalize_tile(t, carry):
-        unit_w = unit_rows(proto_ref[tile_rows(t), :])[0]
-        c_buf[tile_rows(t), :] = unit_w.astype(jnp.bfloat16)
-        ct_buf[:, tile_rows(t)] = unit_w.T.astype(jnp.bfloat16)
-        return carry
-
-    lax.fori_loop(0, tiles, normalize_tile, 0, unroll=True)
-
-    for dz in range(1, n_z):
-        s1[dz - 1].wait_recv()
-        send_shard(dz)
     code_copies = []
     for d in range(1, n_plane):
         q, device = plane_peer(d)
@@ -159,6 +147,20 @@
         code_copies[-1].start()
     sent += code_copies
 
+    def tile_rows(t):
+        return pl.ds(pl.multiple_of(t * tile, tile), tile)
+
+    def normalize_tile(t, carry):
+        unit_w = unit_rows(proto_ref[tile_rows(t), :])[0]
+        c_buf[tile_rows(t), :] = unit_w.astype(jnp.bfloat16)
+        ct_buf[:, tile_rows(t)] = unit_w.T.astype(jnp.bfloat16)
+        return carry
+
+    lax.fori_loop(0, tiles, normalize_tile, 0, unroll=True)
+
+    for dz in range(1, n_z):
+        s1[dz - 1].wait_recv()
+        send_shard(dz)
     def score_unit(half, q):
         rows = z_all[half, q]
 
@@ -322,6 +324,10 @@
 
     wide = min(owned, 2 * tile)
 
+    def out_copy(t):
+        rows = pl.ds(pl.multiple_of(t * wide, wide), wide)
+        return pltpu.make_async_copy(gp_buf.at[rows, :], gproto_ref.at[rows, :], gp_sem.at[t])
+
     def proto_tile(t, carry):
         rows = pl.ds(pl.multiple_of(t * wide, wide), wide)
         exponents = jnp.concatenate([e_all[u, rows, :] for u in range(2 * n_plane)], axis=1)
@@ -333,7 +339,8 @@
         )
         unit_w, length = unit_rows(proto_ref[rows, :])
         along = jnp.sum(unit_w * grad, axis=-1, keepdims=True)
-        gproto_ref[rows, :] = (grad - unit_w * along) / length
+        gp_buf[rows, :] = (grad - unit_w * along) / length
+        out_copy(t).start()
         return carry
 
     first = (owned // wide) * 3 // 4
@@ -365,6 +372,8 @@
     grad_rows = (score_grad - unit_e * along) / emb_length
     for v in range(crops):
         gemb_ref[:, v, :] = grad_rows[v * images:(v + 1) * images]
+    for t in range(owned // wide):
+        out_copy(t).wait()
     for copy in sent:
         copy.wait_send()
 
@@ -389,6 +398,29 @@
     sems.append(dma)
     for count in (n_proto - 1, n_plane - 1, n_plane, n_plane - 1, n_z - 1):
         sems += [dma((max(count, 1),)), dma((max(count, 1),))]
+    scratch = [
+        pltpu.VMEM((owned, features), f32),
+        dma((max(owned // (2 * tile), 1),)),
+        pltpu.VMEM((2, n_plane, unit, features), bf16),
+        pltpu.VMEM((n_plane * group, owned), bf16),
+        pltpu.VMEM((owned, features), bf16),
+        pltpu.VMEM((features, owned), bf16),
+        pltpu.VMEM((units, owned, unit), bf16),
+        pltpu.VMEM((units, unit), f32),
+        pltpu.VMEM((n_proto - 1, units, unit), f32),
+        pltpu.VMEM((units, unit), f32),
+        pltpu.VMEM((max(n_plane - 1, 1), units, unit), f32),
+        pltpu.VMEM((units, unit, features), f32),
+        pltpu.VMEM((n_plane * group, features), f32),
+        pltpu.VMEM((n_dp, n_crop, group, features), bf16),
+        pltpu.VMEM((n_plane, unit, features), f32),
+        pltpu.VMEM((max(n_plane - 1, 1), unit, features), bf16),
+        pltpu.VMEM((max(n_plane - 1, 1), unit, features), bf16),
+        pltpu.VMEM((unit, features), f32),
+        pltpu.VMEM((max(n_z - 1, 1), shard, features), f32),
+    ]
+    held = sum(math.prod(x.shape) * jnp.dtype(x.dtype).itemsize for x in [scratch[0]] + scratch[2:])
+    grant = min(62 * 2**20, held * 5 // 4 + 8 * 2**20)
     grad_emb, grad_proto = pl.pallas_call(
         functools.partial(kernel, (n_dp, n_proto, n_crop, images, crops, tile)),
         out_shape=(
@@ -396,28 +428,10 @@
             jax.ShapeDtypeStruct((owned, features), f32),
         ),
         in_specs=[vmem, pl.BlockSpec(memory_space=pl.ANY), vmem],
-        out_specs=(vmem, vmem),
-        scratch_shapes=[
-            pltpu.VMEM((2, n_plane, unit, features), bf16),
-            pltpu.VMEM((n_plane * group, owned), bf16),
-            pltpu.VMEM((owned, features), bf16),
-            pltpu.VMEM((features, owned), bf16),
-            pltpu.VMEM((units, owned, unit), bf16),
-            pltpu.VMEM((units, unit), f32),
-            pltpu.VMEM((n_proto - 1, units, unit), f32),
-            pltpu.VMEM((units, unit), f32),
-            pltpu.VMEM((max(n_plane - 1, 1), units, unit), f32),
-            pltpu.VMEM((units, unit, features), f32),
-            pltpu.VMEM((n_plane * group, features), f32),
-            pltpu.VMEM((n_dp, n_crop, group, features), bf16),
-            pltpu.VMEM((n_plane, unit, features), f32),
-            pltpu.VMEM((max(n_plane - 1, 1), unit, features), bf16),
-            pltpu.VMEM((max(n_plane - 1, 1), unit, features), bf16),
-            pltpu.VMEM((unit, features), f32),
-            pltpu.VMEM((max(n_z - 1, 1), shard, features), f32),
-        ] + sems,
+        out_specs=(vmem, pl.BlockSpec(memory_space=pl.ANY)),
+        scratch_shapes=scratch + sems,
         compiler_params=pltpu.CompilerParams(
-            collective_id=0, has_side_effects=True, vmem_limit_bytes=62 * 2**20
+            collective_id=0, has_side_effects=True, vmem_limit_bytes=grant
         ),
         cost_estimate=pl.CostEstimate(
             flops=6 * units * unit * owned * features, bytes_accessed=8 * owned * features,

time: 62.8 us -> 71.6 us (1.14)
  Pallas kernels: 57.4 us -> 65.1 us
  local copies, waits for them, and re-layouts: 4.52 us -> 5.52 us
    pallas_call x1, Pallas kernels: 57.4 us -> 65.1 us  [on_device(): pl.pallas_call(functools.partial(kernel, (n_dp, n_proto, n_crop, images,...]
    unnamed x2 -> x8, local copies, waits for them, and re-layouts: 4.52 us -> 5.52 us
where the time goes in v3:
time: 71.6 us; the launch traced here: 71.3 us
  Pallas kernels  65.1 us (91%)
  local copies, waits for them, and re-layouts  5.52 us (8%)
    pallas_call x1, Pallas kernels, on_device(): pl.pallas_call(functools.partial(kernel, (n_dp, n_proto, n_crop, images,...  65.1 us
    unnamed x8, local copies, waits for them, and re-layouts  5.52 us

profile of v3, /device:TPU:0, one launch (start us, length us, event | category | flops | bytes accessed | tf_op | source)
XLA Modules:
  0.0 71.3 jit_solution(13023568864638521223)
XLA Ops:
  0.6 0.0 copy-start
  0.6 1.6 %copy-done = bf16[128,1,8192]{2,0,1:T(8,128)(2,1)S(1)} copy-done((bf16[128,1,8192]{2,0,1:T(8,128)(2,1)S(1)}, bf16[128,1,8192]{2,0,1:T(8,128)(2,1)}, u32[]{:S(2)}) %copy-start) | copy-done | bytes 2097176
  2.2 0.0 copy-start.1
  2.2 1.2 %copy-done.1 = bf16[1,2048,256]{2,1,0:T(8,128)(2,1)S(1)} copy-done((bf16[1,2048,256]{2,1,0:T(8,128)(2,1)S(1)}, bf16[1,2048,256]{2,1,0:T(8,128)(2,1)}, u32[]{:S(2)}) %copy-start.1) | copy-done | bytes 1048600
  3.4 0.0 copy-start.2
  3.4 0.8 %copy-done.2 = bf16[16,1,4,256]{3,2,1,0:T(4,128)(2,1)S(1)} copy-done((bf16[16,1,4,256]{3,2,1,0:T(4,128)(2,1)S(1)}, bf16[16,1,4,256]{3,2,1,0:T(4,128)(2,1)}, u32[]{:S(2)}) %copy-start.2) | copy-done | bytes 32792
  4.2 65.1 %shard_map.50 = (f32[16,4,256]{2,1,0:T(4,128)S(1)}, f32[2048,256]{1,0:T(8,128)S(1)}) custom-call(bf16[16,4,256]{2,1,0:T(4,128)(2,1)S(1)} %bitcast.11, bf16[128,8192]{1,0:T(8,128)(2,1)S(1)} %bitcast.9, bf16[2048,256]{1,0:T(8,128)(2,1)S(1)} %bitcast.10), custom_call_target="tpu_custom_call" | custom-call | flops 6442450944 | bytes 4194304 | tf_op jit(solution)/shard_map/pallas_call | solution.py:424
  69.4 0.6 copy.8
  70.0 1.3 %copy.9 = f32[1,2048,256]{2,1,0:T(8,128)} copy(f32[1,2048,256]{2,1,0:T(8,128)S(1)} %bitcast.7) | data formatting | bytes 4194304
Async XLA Ops:
  0.6 1.6 %copy-start = (bf16[128,1,8192]{2,0,1:T(8,128)(2,1)S(1)}, bf16[128,1,8192]{2,0,1:T(8,128)(2,1)}, u32[]{:S(2)}) copy-start(bf16[128,1,8192]{2,0,1:T(8,128)(2,1)} %param.4) | copy-start | bytes 6291460
  2.2 1.2 %copy-start.1 = (bf16[1,2048,256]{2,1,0:T(8,128)(2,1)S(1)}, bf16[1,2048,256]{2,1,0:T(8,128)(2,1)}, u32[]{:S(2)}) copy-start(bf16[1,2048,256]{2,1,0:T(8,128)(2,1)} %param.5) | copy-start | bytes 3145732
  3.4 0.8 %copy-start.2 = (bf16[16,1,4,256]{3,2,1,0:T(4,128)(2,1)S(1)}, bf16[16,1,4,256]{3,2,1,0:T(4,128)(2,1)}, u32[]{:S(2)}) copy-start(bf16[16,1,4,256]{3,2,1,0:T(4,128)(2,1)} %param.3) | copy-start | bytes 98308
